TPU v7x, 256 devices: a whole 4x4x8 slice. The times are simulated.
256 devices in a mesh: row: 4 (over x_hi, core), rad: 2 (over x_lo), azi: 32 (over z, y).
Axes of the slice: x: 4 (x_hi: 2, x_lo: 2; x = x_hi * 2 + x_lo), y: 4, z: 8, core: 2. Of those that a mesh axis runs over, the one named last changes fastest.
Arguments:
- density: float32 [64, 32, 8192], P('row', 'rad', 'azi'), may hold values from 0.8 to 1.25
- velocity: float32 [3, 64, 32, 8192], P(None, 'row', 'rad', 'azi'), may hold values from -1.2 to 1.2
- pressure: float32 [64, 32, 8192], P('row', 'rad', 'azi'), may hold values from 0.6 to 1.4
- nu_tilde: float32 [64, 32, 8192], P('row', 'rad', 'azi'), may hold values from 0.02 to 0.2
- wall_distance: float32 [64, 32, 8192], P('row', 'rad', 'azi'), may hold values from 0.5 to 4
- interp_fwd: float32 [32, 32], P('rad')
- interp_back: float32 [32, 32], P('rad')
- offset: int32 [1], replicated, may hold values from 0 to 8191
Outputs:
- flow_next: float32 [6, 64, 32, 8192], P(None, 'row', 'rad', 'azi')
- shielding: float32 [64, 32, 8192], P('row', 'rad', 'azi')
All inputs are finite; a program needn't handle non-finite values.
Results may differ from a plain program's by a relative error of at most 0.00005.
Values sent between devices are 32-bit elements; how exact they have to be, the bound alone decides.
No kernel may reach another device: no remote copies, remote signals or barrier semaphores. Data moves between devices by JAX's collectives and lax.ppermute only.
A program may use at most 128 MiB of HBM per device.

v0:
```python
import jax
import jax.numpy as jnp
from jax import lax
from jax.sharding import PartitionSpec as P

GAMMA = 1.4
CFL = 0.8
KAPPA = 0.41
C_DES = 0.65
CB1 = 0.1355
CW1 = 3.239
NU_LAM = 0.001
GRAD_FLOOR = 0.2


def from_behind(block, axis, distance):
    devices = range(lax.axis_size(axis))
    route = [((i - distance) % len(devices), i) for i in devices]
    return lax.ppermute(block, axis, route)


def with_halo(array, sides, width):
    for axis, dim in sides:
        size, length = (lax.axis_size(axis), array.shape[dim])
        up = [(i, (i + 1) % size) for i in range(size)]
        down = [(j, i) for i, j in up]
        last = lax.slice_in_dim(array, length - width, length, axis=dim)
        first = lax.slice_in_dim(array, 0, width, axis=dim)
        before = lax.ppermute(last, axis, up)
        after = lax.ppermute(first, axis, down)
        array = jnp.concatenate([before, array, after], axis=dim)
    return array


def conserved(prim):
    rho = prim[0]
    energy = prim[4] / (GAMMA - 1.0) + 0.5 * rho * (prim[1] ** 2 + prim[2] ** 2 + prim[3] ** 2)
    return jnp.stack([rho, rho * prim[1], rho * prim[2], rho * prim[3], energy, rho * prim[5]], 0)


def normal_flux(prim, direction):
    cons = conserved(prim)
    normal = prim[1 + direction]
    press = prim[4]
    flux = cons * normal[None]
    extra = [jnp.zeros_like(press)] * 6
    extra[1 + direction] = press
    extra[4] = press * normal
    flux = flux + jnp.stack(extra, 0)
    speed = jnp.abs(normal) + jnp.sqrt(GAMMA * press / prim[0])
    return (cons, flux, speed)


def rusanov(left, right, direction):
    cons_l, flux_l, speed_l = normal_flux(left, direction)
    cons_r, flux_r, speed_r = normal_flux(right, direction)
    return 0.5 * (flux_l + flux_r) - 0.5 * jnp.maximum(speed_l, speed_r)[None] * (cons_r - cons_l)


def divergence(padded, direction, axis):
    count = padded.shape[axis]
    left = lax.slice_in_dim(padded, 0, count - 1, axis=axis)
    right = lax.slice_in_dim(padded, 1, count, axis=axis)
    faces = rusanov(left, right, direction)
    return lax.slice_in_dim(faces, 1, count - 1, axis=axis) - lax.slice_in_dim(
        faces, 0, count - 2, axis=axis
    )


def grad_squares(padded, axis):
    count = padded.shape[axis]
    upper = lax.slice_in_dim(padded[1:4], 2, count, axis=axis)
    lower = lax.slice_in_dim(padded[1:4], 0, count - 2, axis=axis)
    return jnp.sum((0.5 * (upper - lower)) ** 2, axis=0)


def speed_bound(prim):
    return (
        jnp.abs(prim[1])
        + jnp.abs(prim[2])
        + jnp.abs(prim[3])
        + 3.0 * jnp.sqrt(GAMMA * prim[4] / prim[0])
    )


def update(prim, flux_sum, grad2, wall_distance, step_size):
    rho = prim[0]
    nut = prim[5]
    strain = jnp.maximum(jnp.sqrt(grad2), GRAD_FLOOR)
    ratio = (nut + NU_LAM) / (KAPPA * KAPPA * wall_distance * wall_distance * strain)
    shielding = 1.0 - jnp.tanh((8.0 * ratio) ** 3)
    length = wall_distance - shielding * jnp.maximum(0.0, wall_distance - C_DES)
    source = rho * (CB1 * strain * nut - CW1 * (nut / length) ** 2)
    state = conserved(prim) - step_size * flux_sum
    state = jnp.concatenate([state[:5], (state[5] + step_size * source)[None]], 0)
    return (state, shielding)


def rotate_plane(plane, amount, width, cycle):
    blocks = amount // width
    rest = amount % width

    def one_block(step, current):
        shifted = from_behind(current, "azi", 1)
        return jnp.where(step < blocks, shifted, current)

    moved = lax.fori_loop(0, cycle - 1, one_block, plane)
    previous = from_behind(moved, "azi", 1)
    joined = jnp.concatenate([previous, moved], 2)
    return lax.dynamic_slice_in_dim(joined, width - rest, width, 2)


def body(density, velocity, pressure, nu_tilde, wall_distance, interp_fwd, interp_back, offset):
    prim = jnp.concatenate([density[None], velocity, pressure[None], nu_tilde[None]], 0)
    rows = lax.axis_size("row")
    cycle = lax.axis_size("azi")
    rads = lax.axis_size("rad")
    row_index = lax.axis_index("row")
    rad_index = lax.axis_index("rad")
    width = prim.shape[3]
    axial_ext = with_halo(prim, (("row", 1),), 1)
    radial_ext = with_halo(prim, (("rad", 2),), 1)
    cycle_pad = with_halo(prim, (("azi", 3),), 1)
    below = axial_ext[:, 0]
    above = axial_ext[:, -1]
    middle = rows // 2
    on_stator = row_index == middle
    on_rotor = row_index == middle - 1
    plane = jnp.where(on_stator, below, above)
    total = width * cycle
    shift_total = offset[0]
    amount = jnp.where(on_stator, shift_total, (total - shift_total) % total)
    rotated = rotate_plane(plane, amount, width, cycle)
    weights = jnp.where(on_stator, interp_fwd, interp_back)
    ghost = jnp.einsum(
        "rk,vkt->vrt",
        weights,
        lax.all_gather(rotated, "rad", axis=1, tiled=True),
        precision=lax.Precision.HIGHEST,
    )
    lower = jnp.where(row_index == 0, prim[:, 0], jnp.where(on_stator, ghost, below))
    upper = jnp.where(row_index == rows - 1, prim[:, -1], jnp.where(on_rotor, ghost, above))
    axial_pad = jnp.concatenate([lower[:, None], prim, upper[:, None]], 1)
    flip = jnp.array([1.0, 1.0, -1.0, 1.0, 1.0, 1.0], dtype=jnp.float32).reshape(6, 1, 1)
    hub_side = jnp.where(rad_index == 0, prim[:, :, 0] * flip, radial_ext[:, :, 0])
    case_side = jnp.where(rad_index == rads - 1, prim[:, :, -1] * flip, radial_ext[:, :, -1])
    radial_pad = jnp.concatenate([hub_side[:, :, None], prim, case_side[:, :, None]], 2)
    largest = lax.pmax(jnp.max(speed_bound(prim)), ("row", "rad", "azi"))
    flux_sum = (
        divergence(axial_pad, 0, 1) + divergence(radial_pad, 1, 2) + divergence(cycle_pad, 2, 3)
    )
    grad2 = grad_squares(axial_pad, 1) + grad_squares(radial_pad, 2) + grad_squares(cycle_pad, 3)
    step_size = CFL / largest
    return update(prim, flux_sum, grad2, wall_distance, step_size)


def solution(mesh):
    placed = (
        P("row", "rad", "azi"),
        P(None, "row", "rad", "azi"),
        P("row", "rad", "azi"),
        P("row", "rad", "azi"),
        P("row", "rad", "azi"),
        P("rad", None),
        P("rad", None),
        P(),
    )
    return jax.shard_map(
        body,
        mesh=mesh,
        in_specs=placed,
        out_specs=(P(None, "row", "rad", "azi"), P("row", "rad", "azi")),
        check_vma=False,
    )
```

profile of v0, /device:TPU:4, one launch (start us, length us, event | category | flops | bytes accessed | tf_op | source)
XLA Modules:
  0.0 424.4 jit_solution(15490706350710698898)
XLA Ops:
  23.7 74.3 %pmax.7 = f32[]{:T(128)} all-reduce(f32[]{:T(128)} %fusion.30), channel_id=1, replica_groups=mesh['row'=4,'rad'=2,'azi'=32] {'row','rad','azi'}, use_global_device_ids=true, to_apply=%region_1.2 | all-reduce | flops 1 | bytes 8 | tf_op jit(solution)/shard_map/pmax | solution.py:148
  121.0 277.5 %while.13 = (s32[]{:T(128)}, f32[6,16,256]{2,1,0:T(8,128)S(1)}, s32[]{:T(128)}, s32[]{:T(128)}) while((s32[]{:T(128)}, f32[6,16,256]{2,1,0:T(8,128)S(1)}, s32[]{:T(128)}, s32[]{:T(128)}) %tuple.73), condition=%wide.region_3.4_spmd, body=%wide.region_2.3_spmd.sunk | while | flops 24579 | bytes 688239 | solution.py:107
  121.1 8.0 %collective-permute-done = f32[6,16,256]{2,1,0:T(8,128)} collective-permute-done((f32[6,16,256]{2,1,0:T(8,128)S(1)}, f32[6,16,256]{2,1,0:T(8,128)}, u32[]{:S(2)}, u32[]{:S(2)}) %collective-permute-start) | collective-permute-done | bytes 98336 | tf_op jit(solution)/shard_map/while/body/eval_jaxpr/ppermute | solution.py:19
  130.1 8.0 %collective-permute-done = f32[6,16,256]{2,1,0:T(8,128)} collective-permute-done((f32[6,16,256]{2,1,0:T(8,128)S(1)}, f32[6,16,256]{2,1,0:T(8,128)}, u32[]{:S(2)}, u32[]{:S(2)}) %collective-permute-start) | collective-permute-done | bytes 98336 | tf_op jit(solution)/shard_map/while/body/eval_jaxpr/ppermute | solution.py:19
  139.2 8.0 %collective-permute-done = f32[6,16,256]{2,1,0:T(8,128)} collective-permute-done((f32[6,16,256]{2,1,0:T(8,128)S(1)}, f32[6,16,256]{2,1,0:T(8,128)}, u32[]{:S(2)}, u32[]{:S(2)}) %collective-permute-start) | collective-permute-done | bytes 98336 | tf_op jit(solution)/shard_map/while/body/eval_jaxpr/ppermute | solution.py:19
  148.2 8.0 %collective-permute-done = f32[6,16,256]{2,1,0:T(8,128)} collective-permute-done((f32[6,16,256]{2,1,0:T(8,128)S(1)}, f32[6,16,256]{2,1,0:T(8,128)}, u32[]{:S(2)}, u32[]{:S(2)}) %collective-permute-start) | collective-permute-done | bytes 98336 | tf_op jit(solution)/shard_map/while/body/eval_jaxpr/ppermute | solution.py:19
  157.3 8.0 %collective-permute-done = f32[6,16,256]{2,1,0:T(8,128)} collective-permute-done((f32[6,16,256]{2,1,0:T(8,128)S(1)}, f32[6,16,256]{2,1,0:T(8,128)}, u32[]{:S(2)}, u32[]{:S(2)}) %collective-permute-start) | collective-permute-done | bytes 98336 | tf_op jit(solution)/shard_map/while/body/eval_jaxpr/ppermute | solution.py:19
  166.3 8.6 %collective-permute-done = f32[6,16,256]{2,1,0:T(8,128)} collective-permute-done((f32[6,16,256]{2,1,0:T(8,128)S(1)}, f32[6,16,256]{2,1,0:T(8,128)}, u32[]{:S(2)}, u32[]{:S(2)}) %collective-permute-start) | collective-permute-done | bytes 98336 | tf_op jit(solution)/shard_map/while/body/eval_jaxpr/ppermute | solution.py:19
  176.0 8.4 %collective-permute-done = f32[6,16,256]{2,1,0:T(8,128)} collective-permute-done((f32[6,16,256]{2,1,0:T(8,128)S(1)}, f32[6,16,256]{2,1,0:T(8,128)}, u32[]{:S(2)}, u32[]{:S(2)}) %collective-permute-start) | collective-permute-done | bytes 98336 | tf_op jit(solution)/shard_map/while/body/eval_jaxpr/ppermute | solution.py:19
  185.4 8.0 %collective-permute-done = f32[6,16,256]{2,1,0:T(8,128)} collective-permute-done((f32[6,16,256]{2,1,0:T(8,128)S(1)}, f32[6,16,256]{2,1,0:T(8,128)}, u32[]{:S(2)}, u32[]{:S(2)}) %collective-permute-start) | collective-permute-done | bytes 98336 | tf_op jit(solution)/shard_map/while/body/eval_jaxpr/ppermute | solution.py:19
  194.5 8.0 %collective-permute-done = f32[6,16,256]{2,1,0:T(8,128)} collective-permute-done((f32[6,16,256]{2,1,0:T(8,128)S(1)}, f32[6,16,256]{2,1,0:T(8,128)}, u32[]{:S(2)}, u32[]{:S(2)}) %collective-permute-start) | collective-permute-done | bytes 98336 | tf_op jit(solution)/shard_map/while/body/eval_jaxpr/ppermute | solution.py:19
  203.5 8.0 %collective-permute-done = f32[6,16,256]{2,1,0:T(8,128)} collective-permute-done((f32[6,16,256]{2,1,0:T(8,128)S(1)}, f32[6,16,256]{2,1,0:T(8,128)}, u32[]{:S(2)}, u32[]{:S(2)}) %collective-permute-start) | collective-permute-done | bytes 98336 | tf_op jit(solution)/shard_map/while/body/eval_jaxpr/ppermute | solution.py:19
  212.6 8.4 %collective-permute-done = f32[6,16,256]{2,1,0:T(8,128)} collective-permute-done((f32[6,16,256]{2,1,0:T(8,128)S(1)}, f32[6,16,256]{2,1,0:T(8,128)}, u32[]{:S(2)}, u32[]{:S(2)}) %collective-permute-start) | collective-permute-done | bytes 98336 | tf_op jit(solution)/shard_map/while/body/eval_jaxpr/ppermute | solution.py:19
  222.1 8.0 %collective-permute-done = f32[6,16,256]{2,1,0:T(8,128)} collective-permute-done((f32[6,16,256]{2,1,0:T(8,128)S(1)}, f32[6,16,256]{2,1,0:T(8,128)}, u32[]{:S(2)}, u32[]{:S(2)}) %collective-permute-start) | collective-permute-done | bytes 98336 | tf_op jit(solution)/shard_map/while/body/eval_jaxpr/ppermute | solution.py:19
  231.1 8.0 %collective-permute-done = f32[6,16,256]{2,1,0:T(8,128)} collective-permute-done((f32[6,16,256]{2,1,0:T(8,128)S(1)}, f32[6,16,256]{2,1,0:T(8,128)}, u32[]{:S(2)}, u32[]{:S(2)}) %collective-permute-start) | collective-permute-done | bytes 98336 | tf_op jit(solution)/shard_map/while/body/eval_jaxpr/ppermute | solution.py:19
  240.2 8.5 %collective-permute-done = f32[6,16,256]{2,1,0:T(8,128)} collective-permute-done((f32[6,16,256]{2,1,0:T(8,128)S(1)}, f32[6,16,256]{2,1,0:T(8,128)}, u32[]{:S(2)}, u32[]{:S(2)}) %collective-permute-start) | collective-permute-done | bytes 98336 | tf_op jit(solution)/shard_map/while/body/eval_jaxpr/ppermute | solution.py:19
  276.9 8.5 %collective-permute-done = f32[6,16,256]{2,1,0:T(8,128)} collective-permute-done((f32[6,16,256]{2,1,0:T(8,128)S(1)}, f32[6,16,256]{2,1,0:T(8,128)}, u32[]{:S(2)}, u32[]{:S(2)}) %collective-permute-start) | collective-permute-done | bytes 98336 | tf_op jit(solution)/shard_map/while/body/eval_jaxpr/ppermute | solution.py:19
  286.5 8.0 %collective-permute-done = f32[6,16,256]{2,1,0:T(8,128)} collective-permute-done((f32[6,16,256]{2,1,0:T(8,128)S(1)}, f32[6,16,256]{2,1,0:T(8,128)}, u32[]{:S(2)}, u32[]{:S(2)}) %collective-permute-start) | collective-permute-done | bytes 98336 | tf_op jit(solution)/shard_map/while/body/eval_jaxpr/ppermute | solution.py:19
  295.5 8.0 %collective-permute-done = f32[6,16,256]{2,1,0:T(8,128)} collective-permute-done((f32[6,16,256]{2,1,0:T(8,128)S(1)}, f32[6,16,256]{2,1,0:T(8,128)}, u32[]{:S(2)}, u32[]{:S(2)}) %collective-permute-start) | collective-permute-done | bytes 98336 | tf_op jit(solution)/shard_map/while/body/eval_jaxpr/ppermute | solution.py:19
  304.6 8.4 %collective-permute-done = f32[6,16,256]{2,1,0:T(8,128)} collective-permute-done((f32[6,16,256]{2,1,0:T(8,128)S(1)}, f32[6,16,256]{2,1,0:T(8,128)}, u32[]{:S(2)}, u32[]{:S(2)}) %collective-permute-start) | collective-permute-done | bytes 98336 | tf_op jit(solution)/shard_map/while/body/eval_jaxpr/ppermute | solution.py:19
  340.3 8.7 %collective-permute-done = f32[6,16,256]{2,1,0:T(8,128)} collective-permute-done((f32[6,16,256]{2,1,0:T(8,128)S(1)}, f32[6,16,256]{2,1,0:T(8,128)}, u32[]{:S(2)}, u32[]{:S(2)}) %collective-permute-start) | collective-permute-done | bytes 98336 | tf_op jit(solution)/shard_map/while/body/eval_jaxpr/ppermute | solution.py:19
  349.2 8.4 %collective-permute-done = f32[6,16,256]{2,1,0:T(8,128)} collective-permute-done((f32[6,16,256]{2,1,0:T(8,128)S(1)}, f32[6,16,256]{2,1,0:T(8,128)}, u32[]{:S(2)}, u32[]{:S(2)}) %collective-permute-start) | collective-permute-done | bytes 98336 | tf_op jit(solution)/shard_map/while/body/eval_jaxpr/ppermute | solution.py:19
  365.9 8.0 %collective-permute-done = f32[6,16,256]{2,1,0:T(8,128)} collective-permute-done((f32[6,16,256]{2,1,0:T(8,128)S(1)}, f32[6,16,256]{2,1,0:T(8,128)}, u32[]{:S(2)}, u32[]{:S(2)}) %collective-permute-start) | collective-permute-done | bytes 98336 | tf_op jit(solution)/shard_map/while/body/eval_jaxpr/ppermute | solution.py:19
  382.3 8.0 %collective-permute-done = f32[6,16,256]{2,1,0:T(8,128)} collective-permute-done((f32[6,16,256]{2,1,0:T(8,128)S(1)}, f32[6,16,256]{2,1,0:T(8,128)}, u32[]{:S(2)}, u32[]{:S(2)}) %collective-permute-start) | collective-permute-done | bytes 98336 | tf_op jit(solution)/shard_map/while/body/eval_jaxpr/ppermute | solution.py:19
  (209 shorter events, 166.1 us)
Async XLA Ops:
  3.1 97.9 %collective-permute-start.6 = (f32[6,16,16,1]{2,1,3,0:T(8,128)S(1)}, f32[6,16,16,1]{2,1,3,0:T(8,128)S(1)}, u32[]{:S(2)}, u32[]{:S(2)}) collective-permute-start(f32[6,16,16,1]{2,1,3,0:T(8,128)S(1)} %copy.21), channel_id=1, source_target_pairs={{0,1},{1,2},{2,3},{3,4},{4,5},{5,6},{6,7},{7,8},{8,9},{9,10},{10,1... | collective-permute-start | bytes 18440 | tf_op jit(solution)/shard_map/ppermute | solution.py:29
  5.4 97.2 %collective-permute-start.7 = (f32[6,16,16,1]{2,1,3,0:T(8,128)S(1)}, f32[6,16,16,1]{2,1,3,0:T(8,128)S(1)}, u32[]{:S(2)}, u32[]{:S(2)}) collective-permute-start(f32[6,16,16,1]{2,1,3,0:T(8,128)S(1)} %copy.23), channel_id=1, source_target_pairs={{1,0},{2,1},{3,2},{4,3},{5,4},{6,5},{7,6},{8,7},{9,8},{10,9},{11,1... | collective-permute-start | bytes 18440 | tf_op jit(solution)/shard_map/ppermute | solution.py:30
  12.3 104.4 %collective-permute-start.4 = (f32[6,16,1,256]{3,2,0,1:T(1,128)S(1)}, f32[6,16,1,256]{3,2,0,1:T(1,128)}, u32[]{:S(2)}, u32[]{:S(2)}) collective-permute-start(f32[6,16,1,256]{3,2,0,1:T(1,128)S(1)} %pad_maximum_fusion.5), channel_id=1, source_target_pairs={{0,32},{32,0},{1,33},{33,1},{2,34},{34,2},{3,35},{35,3},{4,36},{36... | collective-permute-start | bytes 294920 | tf_op jit(solution)/shard_map/ppermute | solution.py:29
  14.3 105.7 %collective-permute-start.1 = (f32[6,1,16,256]{3,2,0,1:T(8,128)}, f32[6,1,16,256]{3,2,0,1:T(8,128)}, u32[]{:S(2)}, u32[]{:S(2)}) collective-permute-start(f32[6,1,16,256]{3,2,0,1:T(8,128)} %get-tuple-element.117), channel_id=1, source_target_pairs={{0,64},{64,128},{128,192},{192,0},{1,65},{65,129},{129,193},{193,1... | collective-permute-start | bytes 294920 | tf_op jit(solution)/shard_map/ppermute | solution.py:29
  99.4 20.6 %collective-permute-start.2 = (f32[6,1,16,256]{3,2,0,1:T(8,128)}, f32[6,1,16,256]{3,2,0,1:T(8,128)}, u32[]{:S(2)}, u32[]{:S(2)}) collective-permute-start(f32[6,1,16,256]{3,2,0,1:T(8,128)} %get-tuple-element.116), channel_id=1, source_target_pairs={{64,0},{128,64},{192,128},{0,192},{65,1},{129,65},{193,129},{1,193... | collective-permute-start | bytes 294920 | tf_op jit(solution)/shard_map/ppermute | solution.py:30
  117.6 281.2 %collective-permute-start.5 = (f32[6,16,1,256]{3,2,0,1:T(1,128)}, f32[6,16,1,256]{3,2,0,1:T(1,128)}, u32[]{:S(2)}, u32[]{:S(2)}) collective-permute-start(f32[6,16,1,256]{3,2,0,1:T(1,128)} %get-tuple-element.80), channel_id=1, source_target_pairs={{32,0},{0,32},{33,1},{1,33},{34,2},{2,34},{35,3},{3,35},{36,4},{4,... | collective-permute-start | bytes 294920 | tf_op jit(solution)/shard_map/ppermute | solution.py:30
  121.0 8.1 %collective-permute-start = (f32[6,16,256]{2,1,0:T(8,128)S(1)}, f32[6,16,256]{2,1,0:T(8,128)}, u32[]{:S(2)}, u32[]{:S(2)}) collective-permute-start(f32[6,16,256]{2,1,0:T(8,128)S(1)} %get-tuple-element.158), channel_id=1, source_target_pairs={{31,0},{0,1},{1,2},{2,3},{3,4},{4,5},{5,6},{6,7},{7,8},{8,9},{9,10... | collective-permute-start | bytes 294920 | tf_op jit(solution)/shard_map/while/body/eval_jaxpr/ppermute | solution.py:19
  130.0 8.1 %collective-permute-start = (f32[6,16,256]{2,1,0:T(8,128)S(1)}, f32[6,16,256]{2,1,0:T(8,128)}, u32[]{:S(2)}, u32[]{:S(2)}) collective-permute-start(f32[6,16,256]{2,1,0:T(8,128)S(1)} %get-tuple-element.158), channel_id=1, source_target_pairs={{31,0},{0,1},{1,2},{2,3},{3,4},{4,5},{5,6},{6,7},{7,8},{8,9},{9,10... | collective-permute-start | bytes 294920 | tf_op jit(solution)/shard_map/while/body/eval_jaxpr/ppermute | solution.py:19
  139.1 8.1 %collective-permute-start = (f32[6,16,256]{2,1,0:T(8,128)S(1)}, f32[6,16,256]{2,1,0:T(8,128)}, u32[]{:S(2)}, u32[]{:S(2)}) collective-permute-start(f32[6,16,256]{2,1,0:T(8,128)S(1)} %get-tuple-element.158), channel_id=1, source_target_pairs={{31,0},{0,1},{1,2},{2,3},{3,4},{4,5},{5,6},{6,7},{7,8},{8,9},{9,10... | collective-permute-start | bytes 294920 | tf_op jit(solution)/shard_map/while/body/eval_jaxpr/ppermute | solution.py:19
  148.1 8.1 %collective-permute-start = (f32[6,16,256]{2,1,0:T(8,128)S(1)}, f32[6,16,256]{2,1,0:T(8,128)}, u32[]{:S(2)}, u32[]{:S(2)}) collective-permute-start(f32[6,16,256]{2,1,0:T(8,128)S(1)} %get-tuple-element.158), channel_id=1, source_target_pairs={{31,0},{0,1},{1,2},{2,3},{3,4},{4,5},{5,6},{6,7},{7,8},{8,9},{9,10... | collective-permute-start | bytes 294920 | tf_op jit(solution)/shard_map/while/body/eval_jaxpr/ppermute | solution.py:19
  166.3 8.7 %collective-permute-start = (f32[6,16,256]{2,1,0:T(8,128)S(1)}, f32[6,16,256]{2,1,0:T(8,128)}, u32[]{:S(2)}, u32[]{:S(2)}) collective-permute-start(f32[6,16,256]{2,1,0:T(8,128)S(1)} %get-tuple-element.158), channel_id=1, source_target_pairs={{31,0},{0,1},{1,2},{2,3},{3,4},{4,5},{5,6},{6,7},{7,8},{8,9},{9,10... | collective-permute-start | bytes 294920 | tf_op jit(solution)/shard_map/while/body/eval_jaxpr/ppermute | solution.py:19
  175.9 8.5 %collective-permute-start = (f32[6,16,256]{2,1,0:T(8,128)S(1)}, f32[6,16,256]{2,1,0:T(8,128)}, u32[]{:S(2)}, u32[]{:S(2)}) collective-permute-start(f32[6,16,256]{2,1,0:T(8,128)S(1)} %get-tuple-element.158), channel_id=1, source_target_pairs={{31,0},{0,1},{1,2},{2,3},{3,4},{4,5},{5,6},{6,7},{7,8},{8,9},{9,10... | collective-permute-start | bytes 294920 | tf_op jit(solution)/shard_map/while/body/eval_jaxpr/ppermute | solution.py:19
  185.3 8.1 %collective-permute-start = (f32[6,16,256]{2,1,0:T(8,128)S(1)}, f32[6,16,256]{2,1,0:T(8,128)}, u32[]{:S(2)}, u32[]{:S(2)}) collective-permute-start(f32[6,16,256]{2,1,0:T(8,128)S(1)} %get-tuple-element.158), channel_id=1, source_target_pairs={{31,0},{0,1},{1,2},{2,3},{3,4},{4,5},{5,6},{6,7},{7,8},{8,9},{9,10... | collective-permute-start | bytes 294920 | tf_op jit(solution)/shard_map/while/body/eval_jaxpr/ppermute | solution.py:19
  194.4 8.1 %collective-permute-start = (f32[6,16,256]{2,1,0:T(8,128)S(1)}, f32[6,16,256]{2,1,0:T(8,128)}, u32[]{:S(2)}, u32[]{:S(2)}) collective-permute-start(f32[6,16,256]{2,1,0:T(8,128)S(1)} %get-tuple-element.158), channel_id=1, source_target_pairs={{31,0},{0,1},{1,2},{2,3},{3,4},{4,5},{5,6},{6,7},{7,8},{8,9},{9,10... | collective-permute-start | bytes 294920 | tf_op jit(solution)/shard_map/while/body/eval_jaxpr/ppermute | solution.py:19
  203.4 8.1 %collective-permute-start = (f32[6,16,256]{2,1,0:T(8,128)S(1)}, f32[6,16,256]{2,1,0:T(8,128)}, u32[]{:S(2)}, u32[]{:S(2)}) collective-permute-start(f32[6,16,256]{2,1,0:T(8,128)S(1)} %get-tuple-element.158), channel_id=1, source_target_pairs={{31,0},{0,1},{1,2},{2,3},{3,4},{4,5},{5,6},{6,7},{7,8},{8,9},{9,10... | collective-permute-start | bytes 294920 | tf_op jit(solution)/shard_map/while/body/eval_jaxpr/ppermute | solution.py:19
  212.5 8.5 %collective-permute-start = (f32[6,16,256]{2,1,0:T(8,128)S(1)}, f32[6,16,256]{2,1,0:T(8,128)}, u32[]{:S(2)}, u32[]{:S(2)}) collective-permute-start(f32[6,16,256]{2,1,0:T(8,128)S(1)} %get-tuple-element.158), channel_id=1, source_target_pairs={{31,0},{0,1},{1,2},{2,3},{3,4},{4,5},{5,6},{6,7},{7,8},{8,9},{9,10... | collective-permute-start | bytes 294920 | tf_op jit(solution)/shard_map/while/body/eval_jaxpr/ppermute | solution.py:19
  222.0 8.1 %collective-permute-start = (f32[6,16,256]{2,1,0:T(8,128)S(1)}, f32[6,16,256]{2,1,0:T(8,128)}, u32[]{:S(2)}, u32[]{:S(2)}) collective-permute-start(f32[6,16,256]{2,1,0:T(8,128)S(1)} %get-tuple-element.158), channel_id=1, source_target_pairs={{31,0},{0,1},{1,2},{2,3},{3,4},{4,5},{5,6},{6,7},{7,8},{8,9},{9,10... | collective-permute-start | bytes 294920 | tf_op jit(solution)/shard_map/while/body/eval_jaxpr/ppermute | solution.py:19
  231.0 8.1 %collective-permute-start = (f32[6,16,256]{2,1,0:T(8,128)S(1)}, f32[6,16,256]{2,1,0:T(8,128)}, u32[]{:S(2)}, u32[]{:S(2)}) collective-permute-start(f32[6,16,256]{2,1,0:T(8,128)S(1)} %get-tuple-element.158), channel_id=1, source_target_pairs={{31,0},{0,1},{1,2},{2,3},{3,4},{4,5},{5,6},{6,7},{7,8},{8,9},{9,10... | collective-permute-start | bytes 294920 | tf_op jit(solution)/shard_map/while/body/eval_jaxpr/ppermute | solution.py:19
  240.1 8.6 %collective-permute-start = (f32[6,16,256]{2,1,0:T(8,128)S(1)}, f32[6,16,256]{2,1,0:T(8,128)}, u32[]{:S(2)}, u32[]{:S(2)}) collective-permute-start(f32[6,16,256]{2,1,0:T(8,128)S(1)} %get-tuple-element.158), channel_id=1, source_target_pairs={{31,0},{0,1},{1,2},{2,3},{3,4},{4,5},{5,6},{6,7},{7,8},{8,9},{9,10... | collective-permute-start | bytes 294920 | tf_op jit(solution)/shard_map/while/body/eval_jaxpr/ppermute | solution.py:19
  276.8 8.6 %collective-permute-start = (f32[6,16,256]{2,1,0:T(8,128)S(1)}, f32[6,16,256]{2,1,0:T(8,128)}, u32[]{:S(2)}, u32[]{:S(2)}) collective-permute-start(f32[6,16,256]{2,1,0:T(8,128)S(1)} %get-tuple-element.158), channel_id=1, source_target_pairs={{31,0},{0,1},{1,2},{2,3},{3,4},{4,5},{5,6},{6,7},{7,8},{8,9},{9,10... | collective-permute-start | bytes 294920 | tf_op jit(solution)/shard_map/while/body/eval_jaxpr/ppermute | solution.py:19
  304.5 8.5 %collective-permute-start = (f32[6,16,256]{2,1,0:T(8,128)S(1)}, f32[6,16,256]{2,1,0:T(8,128)}, u32[]{:S(2)}, u32[]{:S(2)}) collective-permute-start(f32[6,16,256]{2,1,0:T(8,128)S(1)} %get-tuple-element.158), channel_id=1, source_target_pairs={{31,0},{0,1},{1,2},{2,3},{3,4},{4,5},{5,6},{6,7},{7,8},{8,9},{9,10... | collective-permute-start | bytes 294920 | tf_op jit(solution)/shard_map/while/body/eval_jaxpr/ppermute | solution.py:19
  340.2 8.8 %collective-permute-start = (f32[6,16,256]{2,1,0:T(8,128)S(1)}, f32[6,16,256]{2,1,0:T(8,128)}, u32[]{:S(2)}, u32[]{:S(2)}) collective-permute-start(f32[6,16,256]{2,1,0:T(8,128)S(1)} %get-tuple-element.158), channel_id=1, source_target_pairs={{31,0},{0,1},{1,2},{2,3},{3,4},{4,5},{5,6},{6,7},{7,8},{8,9},{9,10... | collective-permute-start | bytes 294920 | tf_op jit(solution)/shard_map/while/body/eval_jaxpr/ppermute | solution.py:19
  349.1 8.5 %collective-permute-start = (f32[6,16,256]{2,1,0:T(8,128)S(1)}, f32[6,16,256]{2,1,0:T(8,128)}, u32[]{:S(2)}, u32[]{:S(2)}) collective-permute-start(f32[6,16,256]{2,1,0:T(8,128)S(1)} %get-tuple-element.158), channel_id=1, source_target_pairs={{31,0},{0,1},{1,2},{2,3},{3,4},{4,5},{5,6},{6,7},{7,8},{8,9},{9,10... | collective-permute-start | bytes 294920 | tf_op jit(solution)/shard_map/while/body/eval_jaxpr/ppermute | solution.py:19
  398.5 8.2 %collective-permute-start.3 = (f32[6,16,256]{2,1,0:T(8,128)S(1)}, f32[6,16,256]{2,1,0:T(8,128)S(1)}, u32[]{:S(2)}, u32[]{:S(2)}) collective-permute-start(f32[6,16,256]{2,1,0:T(8,128)S(1)} %get-tuple-element.66), channel_id=1, source_target_pairs={{31,0},{0,1},{1,2},{2,3},{3,4},{4,5},{5,6},{6,7},{7,8},{8,9},{9,10... | collective-permute-start | bytes 294920 | tf_op jit(solution)/shard_map/ppermute | solution.py:19
  (35 other events, 220.0 us)
where the time goes:
time: 426 us; the launch traced here: 424 us
  waiting for transfers between devices  254 us (60%)
  blocking collectives  79.6 us (19%)
  other arithmetic  49.4 us (12%)
  local copies, waits for them, and re-layouts  20.4 us (5%)
  starting transfers between devices  16.6 us (4%)
    ppermute x32, waiting for transfers between devices, from_behind(): return lax.ppermute(block, axis, route)  254 us
    pmax x1, blocking collectives, body(): largest = lax.pmax(jnp.max(speed_bound(prim)), ('row', 'rad', 'azi'))  74.3 us
    select_n x31, other arithmetic, one_block(): return jnp.where(step < blocks, shifted, current)  21.4 us
    unnamed x59, local copies, waits for them, and re-layouts  14 us
    ppermute x3, starting transfers between devices, with_halo(): after = lax.ppermute(first, axis, down)  10.8 us
  transfers between devices with their start and end apart: 38, of which 32 were waited for; matrix products, arithmetic and copies ran while one was open for 13% of the time, Pallas kernels for 0%

commit v1 on v0

v1 whole, which is shorter than its diff:
```python
import functools

import jax
import jax.numpy as jnp
from jax import lax
from jax.experimental import pallas as pl
from jax.experimental.pallas import tpu as pltpu
from jax.sharding import PartitionSpec as P

GAMMA = 1.4
CFL = 0.8
KAPPA = 0.41
C_DES = 0.65
CB1 = 0.1355
CW1 = 3.239
NU_LAM = 0.001
GRAD_FLOOR = 0.2

AXES = ("row", "rad", "azi")
LANES = 128
F32 = jnp.float32
VMEM = pl.BlockSpec(memory_space=pltpu.VMEM)
SMEM = pl.BlockSpec(memory_space=pltpu.SMEM)


def params(mib=48):
    return pltpu.CompilerParams(vmem_limit_bytes=mib * 1024 * 1024)


def shaped(*dims):
    return jax.ShapeDtypeStruct(dims, F32)


def sound_speed(rho, press):
    return jnp.sqrt(GAMMA * press / rho)


def energy_of(press, m, u):
    return press * (1.0 / (GAMMA - 1.0)) + 0.5 * (m[0] * u[0] + m[1] * u[1] + m[2] * u[2])


def state_of(prim):
    rho, u, press, nut = prim[0], prim[1:4], prim[4], prim[5]
    m = [rho * v for v in u]
    return dict(
        rho=rho, m=m, u=u, p=press, e=energy_of(press, m, u), n=rho * nut, c=sound_speed(rho, press)
    )


def cons_of(s):
    return [s["rho"], s["m"][0], s["m"][1], s["m"][2], s["e"], s["n"]]


def flux_of(s, k):
    w = s["u"][k]
    mom = [s["m"][k] * s["u"][i] for i in range(3)]
    mom[k] = mom[k] + s["p"]
    return [s["m"][k], mom[0], mom[1], mom[2], (s["e"] + s["p"]) * w, s["n"] * w]


def face_of(left, right, k):
    wave = jnp.maximum(jnp.abs(left["u"][k]) + left["c"], jnp.abs(right["u"][k]) + right["c"])
    return [
        (fl + fr) - wave * (ur - ul)
        for fl, fr, ul, ur in zip(
            flux_of(left, k), flux_of(right, k), cons_of(left), cons_of(right)
        )
    ]


NAMES = ("rho", "u0", "u1", "u2", "p", "m0", "m1", "m2", "e", "n", "c")
PASSED = ("rho", "u0", "u1", "u2", "p", "e", "n", "c")


def pack_state(s):
    return dict(
        rho=s["rho"], u0=s["u"][0], u1=s["u"][1], u2=s["u"][2], p=s["p"], e=s["e"], n=s["n"], c=s["c"]
    )


def unpack_state(d):
    u = [d["u0"], d["u1"], d["u2"]]
    return dict(rho=d["rho"], u=u, m=[d["rho"] * v for v in u], p=d["p"], e=d["e"], n=d["n"], c=d["c"])


def derive_kernel(rho, vel, press, nut, der, core, outer, layer, col_up, col_down, top):
    count, radial, width = rho.shape
    even = lax.axis_index("row") % 2 == 0
    inner_rad = lax.axis_index("rad") == 0
    lane = lax.broadcasted_iota(jnp.int32, (radial, LANES), 1)

    def field(v, a):
        if v == 0:
            return rho[a]
        if v == 4:
            return press[a]
        if v == 5:
            return nut[a]
        return vel[v - 1, a]

    def step(a, best):
        r, p = rho[a], press[a]
        u = [vel[i, a] for i in range(3)]
        m = [r * v for v in u]
        c = sound_speed(r, p)
        der[0, a] = m[0]
        der[1, a] = m[1]
        der[2, a] = m[2]
        der[3, a] = energy_of(p, m, u)
        der[4, a] = r * nut[a]
        der[5, a] = c
        speed = jnp.abs(u[0]) + jnp.abs(u[1]) + jnp.abs(u[2]) + 3.0 * c
        for v in range(6):
            plane = field(v, a)
            layer[v, pl.ds(a, 1), :] = jnp.where(inner_rad, plane[radial - 1 :], plane[:1])
            first, last = plane[:, :LANES], plane[:, width - LANES :]
            here = lane == a
            col_up[v] = jnp.where(here, pltpu.roll(last, a + 1, 1), col_up[v])
            col_down[v] = jnp.where(here, pltpu.roll(first, a, 1), col_down[v])
        return jnp.maximum(best, speed)

    col_up[...] = jnp.zeros(col_up.shape, F32)
    col_down[...] = jnp.zeros(col_down.shape, F32)
    best = lax.fori_loop(0, count, step, jnp.zeros((radial, width), F32))
    for v in range(6):
        low, high = field(v, 0), field(v, count - 1)
        core[v] = jnp.where(even, high, low)
        outer[v] = jnp.where(even, low, high)
    largest = jnp.max(best, axis=0, keepdims=True)
    largest = jnp.max(largest, axis=1, keepdims=True)
    top[...] = jnp.broadcast_to(largest.reshape(1, 1, 1), top.shape)


def shift_kernel(cycle, shift, before, own, out):
    width = own.shape[2]
    row = lax.axis_index("row")
    amount = shift[0] % width
    amount = jnp.where(row == 1, amount, jnp.where(row == 2, width - amount, 0))
    tiles = amount // LANES
    rest = amount % LANES
    lane = lax.broadcasted_iota(jnp.int32, (own.shape[1], LANES), 1)
    for v in range(6):
        parts = [
            pltpu.roll(ref[v, :, h * LANES : (h + 1) * LANES], rest, 1)
            for ref in (before, own)
            for h in range(2)
        ]
        for t in range(2):
            picks = [
                jnp.where(lane < rest, parts[max(1 + t - q, 0)], parts[2 + t - q]) for q in range(3)
            ]
            out[v, :, t * LANES : (t + 1) * LANES] = jnp.where(
                tiles == 0, picks[0], jnp.where(tiles == 1, picks[1], picks[2])
            )


def weight_kernel(fwd, back, own, other, out):
    width = own.shape[2]
    radial = own.shape[1]
    low = lax.axis_index("rad") == 0
    table = jnp.where(lax.axis_index("row") == 1, fwd[...], back[...])
    for v in range(6):
        first = jnp.where(low, own[v], other[v])
        second = jnp.where(low, other[v], own[v])
        plane = jnp.concatenate([first, second], 0)
        out[v] = jnp.dot(
            table, plane, precision=lax.Precision.HIGHEST, preferred_element_type=F32
        )


def main_kernel(
    rho, vel, press, nut, der, wall, core, ghost, outer, layer, col_prev, col_next, col_own, top,
    flow, shield, low_face, lay_hi, lay_lo, lay_u, azi_hi, azi_lo, azi_u,
):
    count, radial, width = rho.shape
    row, rad = lax.axis_index("row"), lax.axis_index("rad")
    even = row % 2 == 0
    at_low = rad == 0
    coupled = (row == 1) | (row == 2)
    sub = lax.broadcasted_iota(jnp.int32, (8, width), 0)
    lane = lax.broadcasted_iota(jnp.int32, (radial, LANES), 1)
    step_size = CFL / jnp.max(top[...])
    half = 0.5 * step_size

    def prims(a):
        return [rho[a], vel[0, a], vel[1, a], vel[2, a], press[a], nut[a]]

    def state_at(a):
        return dict(
            rho=rho[a],
            u=[vel[i, a] for i in range(3)],
            p=press[a],
            m=[der[i, a] for i in range(3)],
            e=der[3, a],
            n=der[4, a],
            c=der[5, a],
        )

    def up_r(v, halo):
        lo, hi = pltpu.roll(v[:8], 7, 0), pltpu.roll(v[8:], 7, 0)
        edge = sub == 7
        return jnp.concatenate([jnp.where(edge, hi, lo), jnp.where(edge, halo, hi)], 0)

    def down_r(v, halo):
        lo, hi = pltpu.roll(v[:8], 1, 0), pltpu.roll(v[8:], 1, 0)
        edge = sub == 0
        return jnp.concatenate([jnp.where(edge, halo, lo), jnp.where(edge, lo, hi)], 0)

    def up_t(v, halo):
        lo, hi = pltpu.roll(v[:, :LANES], LANES - 1, 1), pltpu.roll(v[:, LANES:], LANES - 1, 1)
        edge = lane == LANES - 1
        return jnp.concatenate([jnp.where(edge, hi, lo), jnp.where(edge, halo, hi)], 1)

    def down_t(v, halo):
        lo, hi = pltpu.roll(v[:, :LANES], 1, 1), pltpu.roll(v[:, LANES:], 1, 1)
        edge = lane == 0
        return jnp.concatenate([jnp.where(edge, halo, lo), jnp.where(edge, lo, hi)], 1)

    def edge_layer(r):
        return [rho[:, r, :], vel[0, :, r, :], vel[1, :, r, :], vel[2, :, r, :], press[:, r, :], nut[:, r, :]]

    def mirrored(prim):
        return [prim[0], prim[1], -prim[2], prim[3], prim[4], prim[5]]

    got = [layer[v] for v in range(6)]
    bottom, ceiling = edge_layer(0), edge_layer(radial - 1)
    high = [jnp.where(at_low, g, w) for g, w in zip(got, mirrored(ceiling))]
    low = [jnp.where(at_low, w, g) for g, w in zip(got, mirrored(bottom))]
    high_state = pack_state(state_of(high))
    for i, name in enumerate(PASSED):
        lay_hi[i] = high_state[name]
    for i, f in enumerate(face_of(state_of(low), state_of(bottom), 1)):
        lay_lo[i] = f
    for i in range(3):
        lay_u[i] = low[1 + i]

    nxt = state_of([col_next[v] for v in range(6)])
    nxt_state = pack_state(nxt)
    for i, name in enumerate(PASSED):
        azi_hi[i] = nxt_state[name]
    prev = [col_prev[v] for v in range(6)]
    for i, f in enumerate(face_of(state_of(prev), state_of([col_own[v] for v in range(6)]), 2)):
        azi_lo[i] = f
    for i in range(3):
        azi_u[i] = prev[1 + i]

    def end_prims(is_core, a):
        return [
            jnp.where(is_core, core[v], jnp.where(coupled, ghost[v], outer[v])) for v in range(6)
        ]

    below = end_prims(jnp.logical_not(even), 0)
    above = end_prims(even, count - 1)
    for i, f in enumerate(face_of(state_of(below), state_at(0), 0)):
        low_face[i] = f

    def step(a, _):
        here = state_at(a)
        nut_a = nut[a]
        last = a == count - 1
        first = a == 0
        later = jnp.minimum(a + 1, count - 1)
        earlier = jnp.maximum(a - 1, 0)
        up_prims = [jnp.where(last, g, h) for g, h in zip(above, prims(later))]
        total = [None] * 6
        grad2 = None
        right = state_of(up_prims)
        for i, f in enumerate(face_of(here, right, 0)):
            total[i] = f - low_face[i]
            low_face[i] = f
        for i in range(3):
            down = jnp.where(first, below[1 + i], vel[i, earlier])
            d = up_prims[1 + i] - down
            grad2 = d * d if grad2 is None else grad2 + d * d
        packed = pack_state(here)
        row_of = pl.ds(a, 1)
        shifted = {n: up_r(packed[n], lay_hi[i, row_of, :]) for i, n in enumerate(PASSED)}
        face = face_of(here, unpack_state(shifted), 1)
        for i, f in enumerate(face):
            total[i] = total[i] + (f - down_r(f, lay_lo[i, row_of, :]))
        for i in range(3):
            d = shifted["u%d" % i] - down_r(here["u"][i], lay_u[i, row_of, :])
            grad2 = grad2 + d * d
        to_end = (LANES - 1) - a
        to_start = (LANES - a) % LANES
        shifted = {n: up_t(packed[n], pltpu.roll(azi_hi[i], to_end, 1)) for i, n in enumerate(PASSED)}
        face = face_of(here, unpack_state(shifted), 2)
        for i, f in enumerate(face):
            total[i] = total[i] + (f - down_t(f, pltpu.roll(azi_lo[i], to_start, 1)))
        for i in range(3):
            d = shifted["u%d" % i] - down_t(here["u"][i], pltpu.roll(azi_u[i], to_start, 1))
            grad2 = grad2 + d * d
        dist = wall[a]
        strain = jnp.maximum(jnp.sqrt(0.25 * grad2), GRAD_FLOOR)
        ratio = (nut_a + NU_LAM) / (KAPPA * KAPPA * dist * dist * strain)
        eight = 8.0 * ratio
        shielding = 1.0 - jnp.tanh(eight * eight * eight)
        length = dist - shielding * jnp.maximum(0.0, dist - C_DES)
        quot = nut_a / length
        source = here["rho"] * (CB1 * strain * nut_a - CW1 * (quot * quot))
        cons = cons_of(here)
        for i in range(5):
            flow[i, a] = cons[i] - half * total[i]
        flow[5, a] = cons[5] - half * total[5] + step_size * source
        shield[a] = shielding
        return 0

    lax.fori_loop(0, count, step, 0)


def body(density, velocity, pressure, nu_tilde, wall_distance, interp_fwd, interp_back, offset):
    rows, rads, cycle = (lax.axis_size(n) for n in AXES)
    count, radial, width = density.shape
    devices = rows * rads * cycle

    def device(row, rad, azi):
        return (row * rads + rad) * cycle + azi % cycle

    def everyone(target):
        return [
            (device(r, d, a), target(r, d, a))
            for r in range(rows)
            for d in range(rads)
            for a in range(cycle)
        ]

    plane = shaped(6, radial, width)
    column = shaped(6, radial, LANES)
    der, core, outer, layer, col_up, col_down, top = pl.pallas_call(
        derive_kernel,
        out_shape=(
            shaped(6, count, radial, width), plane, plane, shaped(6, count, width), column, column,
            shaped(devices, 1, LANES),
        ),
        in_specs=[VMEM] * 4,
        out_specs=(VMEM,) * 7,
        compiler_params=params(),
        name="derive",
    )(density, velocity, pressure, nu_tilde)

    up = everyone(lambda r, d, a: device(r, d, a + 1))
    down = everyone(lambda r, d, a: device(r, d, a - 1))
    pair = everyone(lambda r, d, a: device(r ^ 1, d, a))
    across = everyone(lambda r, d, a: device(r, rads - 1 - d, a))
    came = lax.ppermute(jnp.concatenate([outer, col_up], 2), AXES, up)
    col_next = lax.ppermute(col_down, AXES, down)
    core_got = lax.ppermute(core, AXES, pair)
    tops = lax.all_to_all(top, AXES, 0, 0)

    moved = pl.pallas_call(
        functools.partial(shift_kernel, cycle),
        out_shape=plane,
        in_specs=[SMEM, VMEM, VMEM],
        out_specs=VMEM,
        compiler_params=params(),
        name="shift",
    )(offset, came[:, :, :width], outer)
    swapped = lax.ppermute(jnp.concatenate([moved, layer], 1), AXES, across)
    weighted = pl.pallas_call(
        weight_kernel,
        out_shape=plane,
        in_specs=[VMEM] * 4,
        out_specs=VMEM,
        compiler_params=params(),
        name="weigh",
    )(interp_fwd, interp_back, moved, swapped[:, :radial])

    def far(blocks):
        route = []
        for d in range(rads):
            for a in range(cycle):
                route.append((device(1, d, a), device(2, d, a + blocks)))
                route.append((device(2, d, a), device(1, d, a + cycle - 1 - blocks)))
        return lambda block: lax.ppermute(block, AXES, route)

    ghost = lax.switch(offset[0] // width, [far(b) for b in range(cycle)], weighted)

    return pl.pallas_call(
        main_kernel,
        out_shape=(shaped(6, count, radial, width), shaped(count, radial, width)),
        in_specs=[VMEM] * 14,
        out_specs=(VMEM, VMEM),
        scratch_shapes=[
            pltpu.VMEM((6, radial, width), F32),
            pltpu.VMEM((8, count, width), F32),
            pltpu.VMEM((6, count, width), F32),
            pltpu.VMEM((3, count, width), F32),
            pltpu.VMEM((8, radial, LANES), F32),
            pltpu.VMEM((6, radial, LANES), F32),
            pltpu.VMEM((3, radial, LANES), F32),
        ],
        compiler_params=params(),
        name="advance",
    )(
        density, velocity, pressure, nu_tilde, der, wall_distance, core_got, ghost, outer,
        swapped[:, radial:], came[:, :, width:], col_next, col_down, tops,
    )


def solution(mesh):
    placed = (
        P("row", "rad", "azi"),
        P(None, "row", "rad", "azi"),
        P("row", "rad", "azi"),
        P("row", "rad", "azi"),
        P("row", "rad", "azi"),
        P("rad", None),
        P("rad", None),
        P(),
    )
    return jax.shard_map(
        body,
        mesh=mesh,
        in_specs=placed,
        out_specs=(P(None, "row", "rad", "azi"), P("row", "rad", "azi")),
        check_vma=False,
    )
```

time: 426 us -> 62.5 us (0.15)
  the two profiles are of different devices: /device:TPU:4 before, /device:TPU:1 now
where the time goes in v1:
time: 62.5 us; the launch traced here: 63.4 us
  starting transfers between devices  26.7 us (43%)
  waiting for transfers between devices  16.5 us (26%)
  local copies, waits for them, and re-layouts  9.07 us (15%)
  Pallas kernels  8.94 us (14%)
  between operations  1.44 us (2%)
  other arithmetic  0.7 us (1%)
    ppermute x1, waiting for transfers between devices, body(): came = lax.ppermute(jnp.concatenate([outer, col_up], 2), AXES, up)  9.64 us
    all_to_all x1, starting transfers between devices, body(): tops = lax.all_to_all(top, AXES, 0, 0)  9.49 us
    ppermute x1, waiting for transfers between devices, far(): return lambda block: lax.ppermute(block, AXES, route)  6.89 us
    pallas_call x1, Pallas kernels, body(): pl.pallas_call(main_kernel, out_shape=(shaped(6, count, radial, width), s...  6.85 us
    ppermute x1, starting transfers between devices, body(): col_next = lax.ppermute(col_down, AXES, down)  6.72 us
    unnamed x34, local copies, waits for them, and re-layouts  6.66 us
    ppermute x1, starting transfers between devices, far(): return lambda block: lax.ppermute(block, AXES, route)  6.41 us
    ppermute x1, starting transfers between devices, body(): came = lax.ppermute(jnp.concatenate([outer, col_up], 2), AXES, up)  2.2 us
  transfers between devices with their start and end apart: 6, of which 2 were waited for; matrix products, arithmetic and copies ran while one was open for 4% of the time, Pallas kernels for 0%

profile of v1, /device:TPU:1, one launch (start us, length us, event | category | flops | bytes accessed | tf_op | source)
XLA Modules:
  0.0 63.4 jit_solution(14685453736522638847)
XLA Ops:
  0.6 0.0 copy-start
  0.6 1.1 %copy-done = f32[3,16,16,256]{3,2,1,0:T(8,128)S(1)} copy-done((f32[3,16,16,256]{3,2,1,0:T(8,128)S(1)}, f32[3,16,16,256]{3,2,1,0:T(8,128)}, u32[]{:S(2)}) %copy-start) | copy-done | bytes 786456
  1.8 0.9 %copy-done.2 = f32[16,16,256]{2,1,0:T(8,128)S(1)} copy-done((f32[16,16,256]{2,1,0:T(8,128)S(1)}, f32[16,16,256]{2,1,0:T(8,128)}, u32[]{:S(2)}) %copy-start.2) | copy-done | bytes 262168
  2.7 0.9 %copy-done.4 = f32[16,16,256]{2,1,0:T(8,128)S(1)} copy-done((f32[16,16,256]{2,1,0:T(8,128)S(1)}, f32[16,16,256]{2,1,0:T(8,128)}, u32[]{:S(2)}) %copy-start.4) | copy-done | bytes 262168
  3.7 0.9 %copy-done.6 = f32[16,16,256]{2,1,0:T(8,128)S(1)} copy-done((f32[16,16,256]{2,1,0:T(8,128)S(1)}, f32[16,16,256]{2,1,0:T(8,128)}, u32[]{:S(2)}) %copy-start.6) | copy-done | bytes 262168
  4.6 1.7 %derive.1 = (f32[6,16,16,256]{3,2,1,0:T(8,128)S(1)}, f32[6,16,256]{2,1,0:T(8,128)S(1)}, f32[6,16,256]{2,1,0:T(8,128)S(1)}, f32[6,16,256]{2,1,0:T(8,128)S(1)}, f3...) custom-call(f32[16,16,256]{2,1,0:T(8,128)S(1)} %copy-done.2, ...), custom_call_target="tpu_custom_call" | custom-call | tf_op jit(solution)/shard_map/derive/pallas_call | solution.py:329
  6.4 2.2 %collective-permute-start.33 = (f32[6,16,384]{2,1,0:T(8,128)S(1)}, f32[6,16,384]{2,1,0:T(8,128)S(1)}, u32[]{:S(2)}, u32[]{:S(2)}) collective-permute-start(f32[6,16,384]{2,1,0:T(8,128)S(1)} %pad_maximum_fusion.1), channel_id=1, source_target_pairs={{0,1},{1,2},{2,3},{3,4},{4,5},{5,6},{6,7},{7,8},{8,9},{9,10},{10,1... | collective-permute-start | bytes 442376 | tf_op jit(solution)/shard_map/ppermute | solution.py:345
  9.3 9.6 %collective-permute-done.33 = f32[6,16,384]{2,1,0:T(8,128)S(1)} collective-permute-done((f32[6,16,384]{2,1,0:T(8,128)S(1)}, f32[6,16,384]{2,1,0:T(8,128)S(1)}, u32[]{:S(2)}, u32[]{:S(2)}) %collective-permute-start.33) | collective-permute-done | bytes 147488 | tf_op jit(solution)/shard_map/ppermute | solution.py:345
  19.0 0.1 shift.2.own
  19.1 0.7 %pad_maximum_fusion = f32[6,32,256]{2,1,0:T(8,128)} fusion(f32[6,16,256]{2,1,0:T(8,128)S(1)} %get-tuple-element.78, f32[6,16,256]{2,1,0:T(8,128)S(1)} %shift.2.own), kind=kLoop, calls=%fused_computation | loop fusion | flops 49152 | bytes 393216 | tf_op jit(solution)/shard_map/concatenate | solution.py:358
  19.8 1.2 %collective-permute-start.34 = (f32[6,32,256]{2,1,0:T(8,128)}, f32[6,32,256]{2,1,0:T(8,128)}, u32[]{:S(2)}, u32[]{:S(2)}) collective-permute-start(f32[6,32,256]{2,1,0:T(8,128)} %pad_maximum_fusion), channel_id=1, source_target_pairs={{0,32},{1,33},{2,34},{3,35},{4,36},{5,37},{6,38},{7,39},{8,40},{9,... | collective-permute-start | bytes 589832 | tf_op jit(solution)/shard_map/ppermute | solution.py:358
  21.0 9.5 %all-to-all-start = ((f32[256,1,128]{2,1,0:T(1,128)}), f32[256,1,128]{2,1,0:T(1,128)S(1)}, u32[]{:S(2)}, u32[]{:S(2)}) async-start(f32[256,1,128]{2,1,0:T(1,128)} %copy-done.10), calls=%async_computation | async-start | bytes 262144 | tf_op jit(solution)/shard_map/all_to_all | solution.py:348
  30.5 6.7 %collective-permute-start.35 = (f32[6,16,128]{2,1,0:T(8,128)}, f32[6,16,128]{2,1,0:T(8,128)}, u32[]{:S(2)}, u32[]{:S(2)}) collective-permute-start(f32[6,16,128]{2,1,0:T(8,128)} %copy-done.11), channel_id=1, source_target_pairs={{0,31},{1,0},{2,1},{3,2},{4,3},{5,4},{6,5},{7,6},{8,7},{9,8},{10,9... | collective-permute-start | bytes 147464 | tf_op jit(solution)/shard_map/ppermute | solution.py:346
  37.2 0.6 %collective-permute-start.32 = (f32[6,16,256]{2,1,0:T(8,128)}, f32[6,16,256]{2,1,0:T(8,128)}, u32[]{:S(2)}, u32[]{:S(2)}) collective-permute-start(f32[6,16,256]{2,1,0:T(8,128)} %copy-done.15), channel_id=1, source_target_pairs={{0,64},{1,65},{2,66},{3,67},{4,68},{5,69},{6,70},{7,71},{8,72},{9,... | collective-permute-start | bytes 294920 | tf_op jit(solution)/shard_map/ppermute | solution.py:347
  37.9 0.8 %slice.19.col_prev = f32[6,16,128]{2,1,0:T(8,128)S(1)} slice(f32[6,16,384]{2,1,0:T(8,128)} %copy-done.16), slice={[0:6], [0:16], [256:384]} | slice | bytes 98304 | tf_op jit(solution)/shard_map/slice | solution.py:396
  38.7 1.6 %fusion = (f32[6,16,256]{2,1,0:T(8,128)}, f32[6,16,256]{2,1,0:T(8,128)S(1)}) fusion(f32[6,32,256]{2,1,0:T(8,128)} %collective-permute-done.34), kind=kLoop, calls=%fused_computation.2 | loop fusion | bytes 393216 | tf_op jit(solution)/shard_map/slice | solution.py:396
  40.3 0.2 weigh.1
  40.5 13.3 %conditional.1 = (f32[6,16,256]{2,1,0:T(8,128)}) conditional(s32[]{:T(128)} %clamp.3, f32[6,16,256]{2,1,0:T(8,128)S(1)} %weigh.1, f32[6,16,256]{2,1,0:T(8,128)S(1)} %weigh.1, f32[6,16,256]{2,1,0:T(8,128)S(1)} %weigh.1, f32[6,16,256]{2,1,0:T(8,128)S(1)} %weigh.1, f32[6,16,256]{2,1,0:T(8,128)S(1)} %weigh.1, ...), branch_computations={%region_0.1_spmd, %region_1.2_spmd, %region_2.3_spmd, %region_3.4_... | conditional | bytes 393264 | solution.py:376
  40.5 6.4 %collective-permute-start.20 = (f32[6,16,256]{2,1,0:T(8,128)S(1)}, f32[6,16,256]{2,1,0:T(8,128)}, u32[]{:S(2)}, u32[]{:S(2)}) collective-permute-start(f32[6,16,256]{2,1,0:T(8,128)S(1)} %param.20), channel_id=1, source_target_pairs={{64,148},{128,75},{65,149},{129,76},{66,150},{130,77},{67,151},{13... | collective-permute-start | bytes 294920 | tf_op jit(solution)/shard_map/cond/branch_20_fun/ppermute | solution.py:374
  46.9 6.9 %collective-permute-done.20 = f32[6,16,256]{2,1,0:T(8,128)} collective-permute-done((f32[6,16,256]{2,1,0:T(8,128)S(1)}, f32[6,16,256]{2,1,0:T(8,128)}, u32[]{:S(2)}, u32[]{:S(2)}) %collective-permute-start.20) | collective-permute-done | bytes 98336 | tf_op jit(solution)/shard_map/cond/branch_20_fun/ppermute | solution.py:374
  53.9 0.9 %copy-done.8 = f32[6,16,256]{2,1,0:T(8,128)S(1)} copy-done((f32[6,16,256]{2,1,0:T(8,128)S(1)}, f32[6,16,256]{2,1,0:T(8,128)}, u32[]{:S(2)}) %copy-start.8) | copy-done | bytes 98328
  54.8 0.9 %copy-done.9 = f32[16,16,256]{2,1,0:T(8,128)S(1)} copy-done((f32[16,16,256]{2,1,0:T(8,128)S(1)}, f32[16,16,256]{2,1,0:T(8,128)}, u32[]{:S(2)}) %copy-start.9) | copy-done | bytes 262168
  55.7 0.8 %copy-done.12 = f32[6,16,128]{2,1,0:T(8,128)S(1)} copy-done((f32[6,16,128]{2,1,0:T(8,128)S(1)}, f32[6,16,128]{2,1,0:T(8,128)}, u32[]{:S(2)}) %copy-start.12) | copy-done | bytes 49176
  56.5 6.9 %advance.1 = (f32[6,16,16,256]{3,2,1,0:T(8,128)}, f32[16,16,256]{2,1,0:T(8,128)}) custom-call(f32[16,16,256]{2,1,0:T(8,128)S(1)} %copy-done.3, f32[3,16,16,256]{3,2,1,0:T(8,128)S(1)} %copy-done.1, f32[16,16,256]{2,1,0:T(8,128)S(1)} %copy-done.5, f32[16,16,256]{2,1,0:T(8,128)S(1)} %copy-done.7, f32[6,16,16,256]{3,2,1,0:T(8,128)S(1)} %get-tuple-element.74.der, ...), custom_call_target="tpu_custom_call" | custom-call | tf_op jit(solution)/shard_map/advance/pallas_call | solution.py:378
  (32 shorter events, 0.1 us)
Async XLA Ops:
  0.6 1.1 %copy-start = (f32[3,16,16,256]{3,2,1,0:T(8,128)S(1)}, f32[3,16,16,256]{3,2,1,0:T(8,128)}, u32[]{:S(2)}) copy-start(f32[3,16,16,256]{3,2,1,0:T(8,128)} %vel.3) | copy-start | bytes 2359300
  1.8 0.9 %copy-start.2 = (f32[16,16,256]{2,1,0:T(8,128)S(1)}, f32[16,16,256]{2,1,0:T(8,128)}, u32[]{:S(2)}) copy-start(f32[16,16,256]{2,1,0:T(8,128)} %rho.3) | copy-start | bytes 786436
  2.7 0.9 %copy-start.4 = (f32[16,16,256]{2,1,0:T(8,128)S(1)}, f32[16,16,256]{2,1,0:T(8,128)}, u32[]{:S(2)}) copy-start(f32[16,16,256]{2,1,0:T(8,128)} %press.3) | copy-start | bytes 786436
  3.7 0.9 %copy-start.6 = (f32[16,16,256]{2,1,0:T(8,128)S(1)}, f32[16,16,256]{2,1,0:T(8,128)}, u32[]{:S(2)}) copy-start(f32[16,16,256]{2,1,0:T(8,128)} %nut.3) | copy-start | bytes 786436
  4.6 35.7 %copy-start.13 = (f32[16,32]{1,0:T(8,128)S(1)}, f32[16,32]{1,0:T(8,128)}, u32[]{:S(2)}) copy-start(f32[16,32]{1,0:T(8,128)} %fwd.1) | copy-start | bytes 6148
  4.6 35.7 %copy-start.14 = (f32[16,32]{1,0:T(8,128)S(1)}, f32[16,32]{1,0:T(8,128)}, u32[]{:S(2)}) copy-start(f32[16,32]{1,0:T(8,128)} %back.1) | copy-start | bytes 6148
  6.3 3.0 %copy-start.10 = (f32[256,1,128]{2,1,0:T(1,128)}, f32[256,1,128]{2,1,0:T(1,128)S(1)}, u32[]{:S(2)}) copy-start(f32[256,1,128]{2,1,0:T(1,128)S(1)} %get-tuple-element.80) | copy-start | bytes 393220
  6.4 13.4 %copy-start.11 = (f32[6,16,128]{2,1,0:T(8,128)}, f32[6,16,128]{2,1,0:T(8,128)S(1)}, u32[]{:S(2)}) copy-start(f32[6,16,128]{2,1,0:T(8,128)S(1)} %get-tuple-element.79.col_own) | copy-start | bytes 147460
  6.4 14.7 %copy-start.15 = (f32[6,16,256]{2,1,0:T(8,128)}, f32[6,16,256]{2,1,0:T(8,128)S(1)}, u32[]{:S(2)}) copy-start(f32[6,16,256]{2,1,0:T(8,128)S(1)} %get-tuple-element.75) | copy-start | bytes 294916
  6.4 47.5 %copy-start.1 = (f32[3,16,16,256]{3,2,1,0:T(8,128)S(1)}, f32[3,16,16,256]{3,2,1,0:T(8,128)}, u32[]{:S(2)}) copy-start(f32[3,16,16,256]{3,2,1,0:T(8,128)} %vel.3) | copy-start | bytes 2359300
  6.4 47.5 %copy-start.3 = (f32[16,16,256]{2,1,0:T(8,128)S(1)}, f32[16,16,256]{2,1,0:T(8,128)}, u32[]{:S(2)}) copy-start(f32[16,16,256]{2,1,0:T(8,128)} %rho.3) | copy-start | bytes 786436
  6.4 47.5 %copy-start.5 = (f32[16,16,256]{2,1,0:T(8,128)S(1)}, f32[16,16,256]{2,1,0:T(8,128)}, u32[]{:S(2)}) copy-start(f32[16,16,256]{2,1,0:T(8,128)} %press.3) | copy-start | bytes 786436
  6.4 47.5 %copy-start.7 = (f32[16,16,256]{2,1,0:T(8,128)S(1)}, f32[16,16,256]{2,1,0:T(8,128)}, u32[]{:S(2)}) copy-start(f32[16,16,256]{2,1,0:T(8,128)} %nut.3) | copy-start | bytes 786436
  6.4 12.5 %collective-permute-start.33 = (f32[6,16,384]{2,1,0:T(8,128)S(1)}, f32[6,16,384]{2,1,0:T(8,128)S(1)}, u32[]{:S(2)}, u32[]{:S(2)}) collective-permute-start(f32[6,16,384]{2,1,0:T(8,128)S(1)} %pad_maximum_fusion.1), channel_id=1, source_target_pairs={{0,1},{1,2},{2,3},{3,4},{4,5},{5,6},{6,7},{7,8},{8,9},{9,10},{10,1... | collective-permute-start | bytes 442376 | tf_op jit(solution)/shard_map/ppermute | solution.py:345
  18.9 2.1 %copy-start.16 = (f32[6,16,384]{2,1,0:T(8,128)}, f32[6,16,384]{2,1,0:T(8,128)S(1)}, u32[]{:S(2)}) copy-start(f32[6,16,384]{2,1,0:T(8,128)S(1)} %collective-permute-done.33) | copy-start | bytes 442372
  19.8 18.9 %collective-permute-start.34 = (f32[6,32,256]{2,1,0:T(8,128)}, f32[6,32,256]{2,1,0:T(8,128)}, u32[]{:S(2)}, u32[]{:S(2)}) collective-permute-start(f32[6,32,256]{2,1,0:T(8,128)} %pad_maximum_fusion), channel_id=1, source_target_pairs={{0,32},{1,33},{2,34},{3,35},{4,36},{5,37},{6,38},{7,39},{8,40},{9,... | collective-permute-start | bytes 589832 | tf_op jit(solution)/shard_map/ppermute | solution.py:358
  21.0 32.8 %all-to-all-start = ((f32[256,1,128]{2,1,0:T(1,128)}), f32[256,1,128]{2,1,0:T(1,128)S(1)}, u32[]{:S(2)}, u32[]{:S(2)}) async-start(f32[256,1,128]{2,1,0:T(1,128)} %copy-done.10), calls=%async_computation | async-start | bytes 262144 | tf_op jit(solution)/shard_map/all_to_all | solution.py:348
  30.5 23.3 %collective-permute-start.35 = (f32[6,16,128]{2,1,0:T(8,128)}, f32[6,16,128]{2,1,0:T(8,128)}, u32[]{:S(2)}, u32[]{:S(2)}) collective-permute-start(f32[6,16,128]{2,1,0:T(8,128)} %copy-done.11), channel_id=1, source_target_pairs={{0,31},{1,0},{2,1},{3,2},{4,3},{5,4},{6,5},{7,6},{8,7},{9,8},{10,9... | collective-permute-start | bytes 147464 | tf_op jit(solution)/shard_map/ppermute | solution.py:346
  37.2 16.6 %collective-permute-start.32 = (f32[6,16,256]{2,1,0:T(8,128)}, f32[6,16,256]{2,1,0:T(8,128)}, u32[]{:S(2)}, u32[]{:S(2)}) collective-permute-start(f32[6,16,256]{2,1,0:T(8,128)} %copy-done.15), channel_id=1, source_target_pairs={{0,64},{1,65},{2,66},{3,67},{4,68},{5,69},{6,70},{7,71},{8,72},{9,... | collective-permute-start | bytes 294920 | tf_op jit(solution)/shard_map/ppermute | solution.py:347
  40.5 13.3 %collective-permute-start.20 = (f32[6,16,256]{2,1,0:T(8,128)S(1)}, f32[6,16,256]{2,1,0:T(8,128)}, u32[]{:S(2)}, u32[]{:S(2)}) collective-permute-start(f32[6,16,256]{2,1,0:T(8,128)S(1)} %param.20), channel_id=1, source_target_pairs={{64,148},{128,75},{65,149},{129,76},{66,150},{130,77},{67,151},{13... | collective-permute-start | bytes 294920 | tf_op jit(solution)/shard_map/cond/branch_20_fun/ppermute | solution.py:374
  53.9 0.9 %copy-start.8 = (f32[6,16,256]{2,1,0:T(8,128)S(1)}, f32[6,16,256]{2,1,0:T(8,128)}, u32[]{:S(2)}) copy-start(f32[6,16,256]{2,1,0:T(8,128)} %get-tuple-element.81.layer) | copy-start | bytes 294916
  54.8 0.9 %copy-start.9 = (f32[16,16,256]{2,1,0:T(8,128)S(1)}, f32[16,16,256]{2,1,0:T(8,128)}, u32[]{:S(2)}) copy-start(f32[16,16,256]{2,1,0:T(8,128)} %wall.1) | copy-start | bytes 786436
  55.7 0.8 %copy-start.12 = (f32[6,16,128]{2,1,0:T(8,128)S(1)}, f32[6,16,128]{2,1,0:T(8,128)}, u32[]{:S(2)}) copy-start(f32[6,16,128]{2,1,0:T(8,128)} %copy-done.11) | copy-start | bytes 147460
